TPU v7x, 32 devices: a whole 2x2x4 slice. The times are simulated.
32 devices in a mesh: groups: 2 (over x), gx: 16 (over z, y, core).
Axes of the slice: x: 2, y: 2, z: 4, core: 2. Of those that a mesh axis runs over, the one named last changes fastest.
Arguments:
- oxygen: float32 [256, 32, 1024], P(('groups', 'gx')), parts along dimension 0, may hold values from 0.4 to 1
- potential: float32 [256, 32, 1024], P(('groups', 'gx')), parts along dimension 0, may hold values from -0.5 to 0.5
- moisture: float32 [256, 32, 1024], P(('groups', 'gx')), parts along dimension 0, may hold values from 0 to 0.2
- rate_constant: float32 [256, 32, 1024], P(('groups', 'gx')), parts along dimension 0, may hold values from 0.5 to 2
- cell_labels: int32 [256, 32, 1024], P(('groups', 'gx')), parts along dimension 0, may hold values from 0 to 2, as said below
- current_density: float32 [2], P('groups'), parts along dimension 0, may hold values from 0.6 to 1.2
Outputs:
- oxygen_out: float32 [256, 32, 1024], P(('groups', 'gx')), parts along dimension 0
- potential_out: float32 [256, 32, 1024], P(('groups', 'gx')), parts along dimension 0
- moisture_out: float32 [256, 32, 1024], P(('groups', 'gx')), parts along dimension 0
There are 2 independent parts, one for each index of `groups`. A program takes and returns all parts, laid end to end along the dimension named above; each array names one. Nothing has to cross between parts.
Inputs may be any that keep to these rules, and one draw needn't show every extreme that they name: `cell_labels`: each cell is 0 (solid carbon), 1 (pore) or 2 (ionomer-covered wall); the shares of pore and wall cells differ between bricks of 8 rows along the first dimension.
All inputs are finite; a program needn't handle non-finite values.
Results may differ from a plain program's by a relative error of at most 0.0001.
Values sent between devices are 32-bit elements; how exact they have to be, the bound alone decides.
A program may use at most 64 MiB of HBM per device.

v0:
```python
import jax
import jax.numpy as jnp
from jax import lax
from jax.sharding import PartitionSpec as P

SUBSTEPS = 2


def padded(block, sides, width):
    for axis, dim in sides:
        count = lax.axis_size(axis)
        forward = [(i, i + 1) for i in range(count - 1)]
        backward = [(target, source) for source, target in forward]
        low = lax.ppermute(
            lax.slice_in_dim(block, block.shape[dim] - width, None, axis=dim), axis, forward
        )
        high = lax.ppermute(lax.slice_in_dim(block, 0, width, axis=dim), axis, backward)
        block = jnp.concatenate([low, block, high], axis=dim)
    return block


def neighbours(field):
    middle = field[1:-1]
    summed = field[2:] + field[:-2]
    padded_z = jnp.pad(middle, ((0, 0), (1, 1), (0, 0)))
    summed = summed + padded_z[:, 2:] + padded_z[:, :-2]
    padded_y = jnp.pad(middle, ((0, 0), (0, 0), (1, 1)))
    return summed + padded_y[:, :, 2:] + padded_y[:, :, :-2]


def diffuse(field, weights):
    return weights[1:-1] * (neighbours(weights * field) - field[1:-1] * neighbours(weights))


def advance(fields, inner_rate, open_m, wall_m, margin_width, electrode_shift, density_value):
    extent = fields.shape[1]
    layers = fields.shape[2]
    oxygen, potential, moisture = (fields[0], fields[1], fields[2])
    own_oxygen = oxygen[margin_width : extent - margin_width]
    own_potential = potential[margin_width : extent - margin_width]
    own_wall = wall_m[margin_width : extent - margin_width]
    overpotential = electrode_shift - own_potential
    forward = jnp.exp(1.5 * overpotential)
    backward = jnp.exp(-1.5 * overpotential)
    resid_part = jnp.sum(
        own_wall * (inner_rate * (own_oxygen * forward - backward) - density_value)
    )
    slope_part = jnp.sum(own_wall * inner_rate * (1.5 * own_oxygen * forward + 1.5 * backward))
    sums_total = lax.psum((resid_part, slope_part), "gx")
    electrode_shift = electrode_shift - sums_total[0] / sums_total[1]
    depth_index = lax.broadcasted_iota(jnp.int32, (1, layers, 1), 1)
    top_m = (depth_index == 0).astype(jnp.float32)
    bottom_m = (depth_index == layers - 1).astype(jnp.float32)
    inner_oxygen = oxygen[1:-1]
    inner_potential = potential[1:-1]
    inner_moisture = moisture[1:-1]
    inner_open = open_m[1:-1]
    inner_wall = wall_m[1:-1]
    overpotential = electrode_shift - inner_potential
    reaction = (
        inner_wall
        * inner_rate
        * (inner_oxygen * jnp.exp(1.5 * overpotential) - jnp.exp(-1.5 * overpotential))
    )
    soaking = 1.0 / (1.0 + moisture * moisture)
    new_oxygen = (
        inner_oxygen
        + 0.16 * diffuse(oxygen, open_m * soaking)
        + 0.16 * top_m * inner_open * (1.0 - inner_oxygen)
        - 0.04 * reaction
    )
    new_potential = (
        inner_potential
        + 0.15 * diffuse(potential, wall_m)
        - 0.15 * bottom_m * inner_wall * inner_potential
        - 0.3 * reaction
    )
    new_moisture = (
        inner_moisture
        + 0.12 * diffuse(moisture, open_m)
        - 0.12 * top_m * inner_open * inner_moisture
        + 0.06 * reaction
    )
    return (jnp.stack([new_oxygen, new_potential, new_moisture]), electrode_shift)


def on_device(oxygen, potential, moisture, rate_constant, cell_labels, current_density):
    rim_depth = 1
    label_ext = padded(cell_labels, (("gx", 0),), rim_depth)
    open_ext = (label_ext >= 1).astype(jnp.float32)
    wall_ext = (label_ext == 2).astype(jnp.float32)
    density_value = current_density[0]
    electrode_shift = jnp.zeros((), jnp.float32)
    fields = jnp.stack([oxygen, potential, moisture])
    for substep in range(SUBSTEPS):
        extended = padded(fields, (("gx", 1),), 1)
        fields, electrode_shift = advance(
            extended, rate_constant, open_ext, wall_ext, 1, electrode_shift, density_value
        )
    return (fields[0], fields[1], fields[2])


def solution(mesh):
    in_specs = (
        P(("groups", "gx"), None, None),
        P(("groups", "gx"), None, None),
        P(("groups", "gx"), None, None),
        P(("groups", "gx"), None, None),
        P(("groups", "gx"), None, None),
        P("groups"),
    )
    out_specs = (
        P(("groups", "gx"), None, None),
        P(("groups", "gx"), None, None),
        P(("groups", "gx"), None, None),
    )
    return jax.shard_map(
        on_device, mesh=mesh, in_specs=in_specs, out_specs=out_specs, check_vma=False
    )
```

profile of v0, /device:TPU:0, one launch (start us, length us, event | category | flops | bytes accessed | tf_op | source)
XLA Modules:
  0.0 132.0 jit_solution(11784845897980141919)
XLA Ops:
  0.6 1.3 %pad_maximum_fusion.7 = (f32[3,1,32,1024]{3,2,1,0:T(8,128)S(1)}, f32[3,1,32,1024]{3,2,1,0:T(8,128)S(1)}) fusion(f32[1,8,32,1024]{3,2,1,0:T(8,128)} %bitcast.49, f32[1,8,32,1024]{3,2,1,0:T(8,128)} %bitcast.47, f32[1,8,32,1024]{3,2,1,0:T(8,128)} %bitcast.45), kind=kLoop, calls=%fused_computation.161 | loop fusion | flops 393216 | bytes 3932160 | tf_op jit(solution)/shard_map/slice | solution.py:15
  2.0 2.4 %collective-permute-start.2 = (f32[3,1,32,1024]{3,2,1,0:T(8,128)S(1)}, f32[3,1,32,1024]{3,2,1,0:T(8,128)S(1)}, u32[]{:S(2)}, u32[]{:S(2)}) collective-permute-start(f32[3,1,32,1024]{3,2,1,0:T(8,128)S(1)} %get-tuple-element.34), channel_id=1, source_target_pairs={{0,1},{1,2},{2,3},{3,4},{4,5},{5,6},{6,7},{7,8},{8,9},{9,10},{10,1... | collective-permute-start | bytes 1179656 | tf_op jit(solution)/shard_map/ppermute | solution.py:14
  4.4 1.3 collective-permute-start.3
  5.7 5.3 %collective-permute-start = (s32[1,32,1024]{2,1,0:T(8,128)S(1)}, s32[1,32,1024]{2,1,0:T(8,128)S(1)}, u32[]{:S(2)}, u32[]{:S(2)}) collective-permute-start(s32[1,32,1024]{2,1,0:T(8,128)S(1)} %get-tuple-element.38), channel_id=1, source_target_pairs={{0,1},{1,2},{2,3},{3,4},{4,5},{5,6},{6,7},{7,8},{8,9},{9,10},{10,1... | collective-permute-start | bytes 393224 | tf_op jit(solution)/shard_map/ppermute | solution.py:14
  11.0 1.3 collective-permute-start.1
  13.1 2.4 %collective-permute-done.1 = s32[1,32,1024]{2,1,0:T(8,128)S(1)} collective-permute-done((s32[1,32,1024]{2,1,0:T(8,128)S(1)}, s32[1,32,1024]{2,1,0:T(8,128)S(1)}, u32[]{:S(2)}, u32[]{:S(2)}) %collective-permute-start.1) | collective-permute-done | bytes 131104 | tf_op jit(solution)/shard_map/ppermute | solution.py:17
  17.4 1.0 copy-done.10
  18.4 1.1 slice.389
  19.6 1.1 slice.393
  20.6 1.1 slice.401
  21.7 1.2 slice.396
  22.9 1.0 slice.406
  24.5 2.6 %multiply_reduce_fusion.2 = (f32[]{:T(128)}, f32[]{:T(128)}, f32[8,32,1024]{2,1,0:T(8,128)}, f32[8,32,1024]{2,1,0:T(8,128)}) fusion(f32[8,32,1024]{2,1,0:T(8,128)S(1)} %copy-done.6, f32[8,32,1024]{2,1,0:T(8,128)S(1)} %copy-done.7, f32[]{:T(128)} %bitcast.37, f32[8,32,1024]{2,1,0:T(8,128)S(1)} %copy-done.20, f32[10,32,1024]{2,1,0:T(8,128)S(1)} %convert_element_type.37), kind=kLoop, calls=%fused_computation.150 | loop fusion | flops 4194302 | bytes 6291468 | tf_op jit(solution)/shard_map/reduce_sum | solution.py:48
  27.1 34.7 %all-reduce.21 = (f32[]{:T(128)}, f32[]{:T(128)}) all-reduce(f32[]{:T(128)} %get-tuple-element.6, f32[]{:T(128)} %get-tuple-element.5), channel_id=1, replica_groups=mesh['groups'=2,'gx'=16] {'gx'}, use_global_device_ids=true, to_apply=%region_1.0 | all-reduce | flops 2 | bytes 16 | tf_op jit(solution)/shard_map/psum | solution.py:49
  63.1 16.0 %multiply_reduce_fusion = (f32[]{:T(128)}, f32[]{:T(128)}, f32[8,32,1024]{2,1,0:T(8,128)S(1)}, f32[8,32,1024]{2,1,0:T(8,128)}, f32[8,32,1024]{2,1,0:T(8,128)S(1)}, /*index=5*/f32[8,32,1024]{2,1,0:T(8,128)S(1)}) fusion(f32[8,32,1024]{2,1,0:T(8,128)} %get-tuple-element.25, f32[]{:T(128)S(6)} %sub.105, f32[]{:T(128)} %bitcast.38, f32[8,32,1024]{2,1,0:T(8,128)} %param.9, ...), kind=kLoop, calls=%fused_computation.145 | loop fusion | flops 16252926 | bytes 23068944 | tf_op jit(solution)/shard_map/reduce_sum | solution.py:48
  79.2 2.6 %fusion.34 = (f32[8,32,1024]{2,1,0:T(8,128)S(1)}, f32[8,32,1024]{2,1,0:T(8,128)}) fusion(f32[8,32,1024]{2,1,0:T(8,128)S(1)} %copy-done.14, f32[8,32,1024]{2,1,0:T(8,128)S(1)} %copy-done.19, f32[10,32,1024]{2,1,0:T(8,128)S(1)} %copy-done.12, f32[8,32,1024]{2,1,0:T(8,128)S(1)} %get-tuple-element.16, f32[32]{0:T(128)S(1)} %compare_select_fusion.1, ...), kind=kLoop, calls=%fused_computation.84 | loop fusion | flops 5242880 | bytes 11534464 | tf_op jit(solution)/shard_map/add | solution.py:79
  81.8 1.0 pad_maximum_fusion.4
  83.0 2.0 %collective-permute-start.4 = (f32[3,1,32,1024]{3,2,1,0:T(8,128)}, f32[3,1,32,1024]{3,2,1,0:T(8,128)}, u32[]{:S(2)}, u32[]{:S(2)}) collective-permute-start(f32[3,1,32,1024]{3,2,1,0:T(8,128)} %get-tuple-element.32), channel_id=1, source_target_pairs={{0,1},{1,2},{2,3},{3,4},{4,5},{5,6},{6,7},{7,8},{8,9},{9,10},{10,1... | collective-permute-start | bytes 1179656 | tf_op jit(solution)/shard_map/ppermute | solution.py:14
  85.0 1.3 collective-permute-start.5
  86.3 31.4 %all-reduce.20 = (f32[]{:T(128)}, f32[]{:T(128)}) all-reduce(f32[]{:T(128)} %get-tuple-element.4, f32[]{:T(128)} %get-tuple-element.3), channel_id=1, replica_groups=mesh['groups'=2,'gx'=16] {'gx'}, use_global_device_ids=true, to_apply=%region_5.6 | all-reduce | flops 2 | bytes 16 | tf_op jit(solution)/shard_map/psum | solution.py:49
  119.1 2.4 %pad_maximum_fusion.1 = f32[3,10,32,1024]{3,2,1,0:T(8,128)S(1)} fusion(f32[3,1,32,1024]{3,2,1,0:T(8,128)} %collective-permute-done.5, f32[1,8,32,1024]{3,2,1,0:T(8,128)} %bitcast.44, f32[1,8,32,1024]{3,2,1,0:T(8,128)} %bitcast.40, f32[1,8,32,1024]{3,2,1,0:T(8,128)} %bitcast.42, f32[3,1,32,1024]{3,2,1,0:T(8,128)} %collective-permute-done.4), kind=kLoop, calls=%fused_computation.1 | loop fusion | flops 3932160 | bytes 7864320 | tf_op jit(solution)/shard_map/concatenate | solution.py:18
  124.9 2.3 %fusion.63 = (f32[8,32,1024]{2,1,0:T(8,128)}, f32[8,32,1024]{2,1,0:T(8,128)S(1)}) fusion(f32[8,32,1024]{2,1,0:T(8,128)S(1)} %copy-done.5, f32[8,32,1024]{2,1,0:T(8,128)S(1)} %slice.423, f32[10,32,1024]{2,1,0:T(8,128)S(1)} %get-tuple-element.30, f32[8,32,1024]{2,1,0:T(8,128)S(1)} %copy-done.17, f32[32]{0:T(128)S(1)} %compare_select_fusion.1, ...), kind=kLoop, calls=%fused_computation.113 | loop fusion | flops 5505024 | bytes 11534468 | tf_op jit(solution)/shard_map/add | solution.py:79
  127.3 2.1 %fusion.55 = f32[8,32,1024]{2,1,0:T(8,128)} fusion(f32[8,32,1024]{2,1,0:T(8,128)S(1)} %copy-done.1, f32[8,32,1024]{2,1,0:T(8,128)S(1)} %slice.420, f32[10,32,1024]{2,1,0:T(8,128)S(1)} %get-tuple-element.31, f32[8,32,1024]{2,1,0:T(8,128)S(1)} %get-tuple-element.12, f32[8,32,1024]{2,1,0:T(8,128)S(1)} %copy-done.16, f32[32]{0:T(128)S(1)} %get-tuple-element.39, ...), kind=kLoop, calls=%fused_computation.105 | loop fusion | flops 3932160 | bytes 8388736 | tf_op jit(solution)/shard_map/sub | solution.py:73
  129.3 2.7 %fusion.44 = f32[8,32,1024]{2,1,0:T(8,128)} fusion(f32[8,32,1024]{2,1,0:T(8,128)S(1)} %copy-done.3, f32[8,32,1024]{2,1,0:T(8,128)S(1)} %slice.410, f32[8,32,1024]{2,1,0:T(8,128)S(1)} %slice.414, f32[10,32,1024]{2,1,0:T(8,128)S(1)} %get-tuple-element.18, f32[10,32,1024]{2,1,0:T(8,128)S(1)} %get-tuple-element.17, f32[8,32,1024]{2,1,0:T(8,128)S(1)} %get-tuple-element.12, ...), kind=kLoop, calls=%fused_computation.94 | loop fusion | flops 5505024 | bytes 10485888 | tf_op jit(solution)/shard_map/sub | solution.py:67
  (64 shorter events, 6.2 us)
Async XLA Ops:
  0.6 5.0 %copy-start.21 = (s32[8,32,1024]{2,1,0:T(8,128)S(1)}, s32[8,32,1024]{2,1,0:T(8,128)}, u32[]{:S(2)}) copy-start(s32[8,32,1024]{2,1,0:T(8,128)} %param.10) | copy-start | bytes 3145732
  2.0 13.5 %collective-permute-start.2 = (f32[3,1,32,1024]{3,2,1,0:T(8,128)S(1)}, f32[3,1,32,1024]{3,2,1,0:T(8,128)S(1)}, u32[]{:S(2)}, u32[]{:S(2)}) collective-permute-start(f32[3,1,32,1024]{3,2,1,0:T(8,128)S(1)} %get-tuple-element.34), channel_id=1, source_target_pairs={{0,1},{1,2},{2,3},{3,4},{4,5},{5,6},{6,7},{7,8},{8,9},{9,10},{10,1... | collective-permute-start | bytes 1179656 | tf_op jit(solution)/shard_map/ppermute | solution.py:14
  4.4 11.1 %collective-permute-start.3 = (f32[3,1,32,1024]{3,2,1,0:T(8,128)S(1)}, f32[3,1,32,1024]{3,2,1,0:T(8,128)S(1)}, u32[]{:S(2)}, u32[]{:S(2)}) collective-permute-start(f32[3,1,32,1024]{3,2,1,0:T(8,128)S(1)} %get-tuple-element.35), channel_id=1, source_target_pairs={{1,0},{2,1},{3,2},{4,3},{5,4},{6,5},{7,6},{8,7},{9,8},{10,9},{11,1... | collective-permute-start | bytes 1179656 | tf_op jit(solution)/shard_map/ppermute | solution.py:17
  5.7 9.8 %copy-start.13 = (f32[8,32,1024]{2,1,0:T(8,128)S(1)}, f32[8,32,1024]{2,1,0:T(8,128)}, u32[]{:S(2)}) copy-start(f32[8,32,1024]{2,1,0:T(8,128)} %param.8) | copy-start | bytes 3145732
  5.7 7.3 %collective-permute-start = (s32[1,32,1024]{2,1,0:T(8,128)S(1)}, s32[1,32,1024]{2,1,0:T(8,128)S(1)}, u32[]{:S(2)}, u32[]{:S(2)}) collective-permute-start(s32[1,32,1024]{2,1,0:T(8,128)S(1)} %get-tuple-element.38), channel_id=1, source_target_pairs={{0,1},{1,2},{2,3},{3,4},{4,5},{5,6},{6,7},{7,8},{8,9},{9,10},{10,1... | collective-permute-start | bytes 393224 | tf_op jit(solution)/shard_map/ppermute | solution.py:14
  11.0 4.5 %collective-permute-start.1 = (s32[1,32,1024]{2,1,0:T(8,128)S(1)}, s32[1,32,1024]{2,1,0:T(8,128)S(1)}, u32[]{:S(2)}, u32[]{:S(2)}) collective-permute-start(s32[1,32,1024]{2,1,0:T(8,128)S(1)} %get-tuple-element.37), channel_id=1, source_target_pairs={{1,0},{2,1},{3,2},{4,3},{5,4},{6,5},{7,6},{8,7},{9,8},{10,9},{11,1... | collective-permute-start | bytes 393224 | tf_op jit(solution)/shard_map/ppermute | solution.py:17
  13.0 2.6 %copy-start.6 = (f32[8,32,1024]{2,1,0:T(8,128)S(1)}, f32[8,32,1024]{2,1,0:T(8,128)}, u32[]{:S(2)}) copy-start(f32[8,32,1024]{2,1,0:T(8,128)} %param.6) | copy-start | bytes 3145732
  13.0 2.6 %copy-start.7 = (f32[8,32,1024]{2,1,0:T(8,128)S(1)}, f32[8,32,1024]{2,1,0:T(8,128)}, u32[]{:S(2)}) copy-start(f32[8,32,1024]{2,1,0:T(8,128)} %param.7) | copy-start | bytes 3145732
  16.7 4.0 %copy-start.8 = (f32[10,32,1024]{2,1,0:T(8,128)}, f32[10,32,1024]{2,1,0:T(8,128)S(1)}, u32[]{:S(2)}) copy-start(f32[10,32,1024]{2,1,0:T(8,128)S(1)} %get-tuple-element.28) | copy-start | bytes 3932164
  16.7 6.2 %copy-start.11 = (f32[10,32,1024]{2,1,0:T(8,128)}, f32[10,32,1024]{2,1,0:T(8,128)S(1)}, u32[]{:S(2)}) copy-start(f32[10,32,1024]{2,1,0:T(8,128)S(1)} %get-tuple-element.23) | copy-start | bytes 3932164
  17.1 2.5 %copy-start.9 = (f32[10,32,1024]{2,1,0:T(8,128)}, f32[10,32,1024]{2,1,0:T(8,128)S(1)}, u32[]{:S(2)}) copy-start(f32[10,32,1024]{2,1,0:T(8,128)S(1)} %get-tuple-element.26) | copy-start | bytes 3932164
  22.9 1.6 %copy-start.20 = (f32[8,32,1024]{2,1,0:T(8,128)S(1)}, f32[8,32,1024]{2,1,0:T(8,128)}, u32[]{:S(2)}) copy-start(f32[8,32,1024]{2,1,0:T(8,128)} %param.9) | copy-start | bytes 3145732
  63.1 16.0 %copy-start.12 = (f32[10,32,1024]{2,1,0:T(8,128)S(1)}, f32[10,32,1024]{2,1,0:T(8,128)}, u32[]{:S(2)}) copy-start(f32[10,32,1024]{2,1,0:T(8,128)} %copy-done.11) | copy-start | bytes 3932164
  63.1 16.0 %copy-start.14 = (f32[8,32,1024]{2,1,0:T(8,128)S(1)}, f32[8,32,1024]{2,1,0:T(8,128)}, u32[]{:S(2)}) copy-start(f32[8,32,1024]{2,1,0:T(8,128)} %param.8) | copy-start | bytes 3145732
  63.1 16.0 %copy-start.18 = (f32[8,32,1024]{2,1,0:T(8,128)S(1)}, f32[8,32,1024]{2,1,0:T(8,128)}, u32[]{:S(2)}) copy-start(f32[8,32,1024]{2,1,0:T(8,128)} %slice.396) | copy-start | bytes 3145732
  63.1 16.0 %copy-start.19 = (f32[8,32,1024]{2,1,0:T(8,128)S(1)}, f32[8,32,1024]{2,1,0:T(8,128)}, u32[]{:S(2)}) copy-start(f32[8,32,1024]{2,1,0:T(8,128)} %slice.406) | copy-start | bytes 3145732
  79.1 2.7 %copy-start = (f32[8,32,1024]{2,1,0:T(8,128)}, f32[8,32,1024]{2,1,0:T(8,128)S(1)}, u32[]{:S(2)}) copy-start(f32[8,32,1024]{2,1,0:T(8,128)S(1)} %get-tuple-element.13) | copy-start | bytes 3145732
  79.1 2.7 %copy-start.2 = (f32[8,32,1024]{2,1,0:T(8,128)}, f32[8,32,1024]{2,1,0:T(8,128)S(1)}, u32[]{:S(2)}) copy-start(f32[8,32,1024]{2,1,0:T(8,128)S(1)} %get-tuple-element.15) | copy-start | bytes 3145732
  83.0 36.0 %collective-permute-start.4 = (f32[3,1,32,1024]{3,2,1,0:T(8,128)}, f32[3,1,32,1024]{3,2,1,0:T(8,128)}, u32[]{:S(2)}, u32[]{:S(2)}) collective-permute-start(f32[3,1,32,1024]{3,2,1,0:T(8,128)} %get-tuple-element.32), channel_id=1, source_target_pairs={{0,1},{1,2},{2,3},{3,4},{4,5},{5,6},{6,7},{7,8},{8,9},{9,10},{10,1... | collective-permute-start | bytes 1179656 | tf_op jit(solution)/shard_map/ppermute | solution.py:14
  85.0 34.0 %collective-permute-start.5 = (f32[3,1,32,1024]{3,2,1,0:T(8,128)}, f32[3,1,32,1024]{3,2,1,0:T(8,128)}, u32[]{:S(2)}, u32[]{:S(2)}) collective-permute-start(f32[3,1,32,1024]{3,2,1,0:T(8,128)} %get-tuple-element.33), channel_id=1, source_target_pairs={{1,0},{2,1},{3,2},{4,3},{5,4},{6,5},{7,6},{8,7},{9,8},{10,9},{11,1... | collective-permute-start | bytes 1179656 | tf_op jit(solution)/shard_map/ppermute | solution.py:17
  122.5 1.8 %copy-start.15 = (f32[8,32,1024]{2,1,0:T(8,128)S(1)}, f32[8,32,1024]{2,1,0:T(8,128)}, u32[]{:S(2)}) copy-start(f32[8,32,1024]{2,1,0:T(8,128)} %get-tuple-element.25) | copy-start | bytes 3145732
  122.6 2.0 %copy-start.1 = (f32[8,32,1024]{2,1,0:T(8,128)S(1)}, f32[8,32,1024]{2,1,0:T(8,128)}, u32[]{:S(2)}) copy-start(f32[8,32,1024]{2,1,0:T(8,128)} %copy-done) | copy-start | bytes 3145732
  122.6 2.3 %copy-start.3 = (f32[8,32,1024]{2,1,0:T(8,128)S(1)}, f32[8,32,1024]{2,1,0:T(8,128)}, u32[]{:S(2)}) copy-start(f32[8,32,1024]{2,1,0:T(8,128)} %copy-done.2) | copy-start | bytes 3145732
  124.9 2.4 %copy-start.16 = (f32[8,32,1024]{2,1,0:T(8,128)S(1)}, f32[8,32,1024]{2,1,0:T(8,128)}, u32[]{:S(2)}) copy-start(f32[8,32,1024]{2,1,0:T(8,128)} %get-tuple-element.14) | copy-start | bytes 3145732
  (4 other events, 5.3 us)
where the time goes:
time: 132 us
  blocking collectives  66 us (50%)
  other arithmetic  35.7 us (27%)
  starting transfers between devices  13.6 us (10%)
  local copies, waits for them, and re-layouts  10 us (8%)
  between operations  4.31 us (3%)
  waiting for transfers between devices  2.39 us (2%)
    psum x2, blocking collectives, advance(): sums_total = lax.psum((resid_part, slope_part), 'gx')  66 us
    reduce_sum x2, other arithmetic, advance(): jnp.sum(own_wall * inner_rate * (1.5 * own_oxygen * forward + 1.5 * backw...  18.6 us
    ppermute x3, starting transfers between devices, padded(): lax.ppermute(lax.slice_in_dim(block, block.shape[dim] - width, None, axis...  9.69 us
    add x2, other arithmetic, advance(): inner_moisture + 0.12 * diffuse(moisture, open_m)  4.96 us
    unnamed x46, local copies, waits for them, and re-layouts  4.1 us
    ppermute x3, starting transfers between devices, padded(): lax.ppermute(lax.slice_in_dim(block, 0, width, axis=dim), axis, backward)  3.86 us
    slice x6, local copies, waits for them, and re-layouts, neighbours(): middle = field[1:-1]  3.5 us
    concatenate x2, other arithmetic, padded(): block = jnp.concatenate([low, block, high], axis=dim)  2.79 us
  transfers between devices with their start and end apart: 6, of which 1 were waited for; matrix products, arithmetic and copies ran while one was open for 0% of the time, Pallas kernels for 0%

commit v1 on v0

v1 whole, which is shorter than its diff:
```python
import functools
import math

import jax
import jax.numpy as jnp
from jax import lax
from jax.experimental import pallas as pl
from jax.experimental.pallas import tpu as pltpu
from jax.sharding import PartitionSpec as P

MESH = pl.DeviceIdType.MESH
LOG = 1.5 * math.log2(math.e)
PAD = 8


def kernel(
    n, rows, layers, width,
    c_in, p_in, m_in, k_in, l_in, density,
    c_out, p_out, m_out,
    c0, p0, m0, q0, lab, c1, p1, m1, q1, rate, fwd, bwd, part, gathered,
    load_sem, store_sem, send_sem, recv_sem, part_send, part_recv,
):
    group = lax.axis_index("groups")
    me = lax.axis_index("gx")
    left, right = lax.rem(me + n - 1, n), lax.rem(me + 1, n)
    tiles = layers // 8
    last = rows + 1
    first = (c0, p0, m0)
    second = (c1, p1, m1)
    ins = (c_in, p_in, m_in, l_in)
    outs = (c_out, p_out, m_out)

    loads = [
        pltpu.make_async_copy(src, dst.at[pl.ds(1, rows), pl.ds(PAD, layers), :], load_sem.at[i])
        for i, (src, dst) in enumerate(((c_in, c0), (p_in, p0), (l_in, lab), (m_in, m0)))
    ]
    loads.append(pltpu.make_async_copy(k_in, rate, load_sem.at[4]))
    for copy in loads:
        copy.start()

    barrier = pltpu.get_barrier_semaphore()

    @pl.loop(1, n)
    def _(d):
        pl.semaphore_signal(
            barrier, inc=1, device_id=(group, lax.rem(me + d, n)), device_id_type=MESH
        )

    def halo(step, way, f, j):
        z = pl.ds(PAD + 8 * j, 8)
        if step == 0:
            src = ins[f].at[0 if way == 0 else rows - 1, pl.ds(8 * j, 8), :]
            dst = (c0, p0, m0, lab)[f]
        else:
            src = second[f].at[1 if way == 0 else rows, z, :]
            dst = second[f]
        return pltpu.make_async_remote_copy(
            src_ref=src,
            dst_ref=dst.at[last if way == 0 else 0, z, :],
            send_sem=send_sem.at[step, way, f, j],
            recv_sem=recv_sem.at[step, way, f, j],
            device_id=(group, left if way == 0 else right),
            device_id_type=MESH,
        )

    has_left = me > 0
    has_right = me < n - 1

    for ref in (c0, p0, m0, q0, lab, c1, p1, m1, q1):
        zero = jnp.zeros((rows + 2, 8, width), ref.dtype)
        ref[:, 0:PAD, :] = zero
        ref[:, PAD + layers :, :] = zero

    @pl.when(jnp.logical_not(has_left))
    def _():
        for ref in (c0, p0, m0, lab, c1, p1, m1):
            ref[0, PAD : PAD + layers, :] = jnp.zeros((layers, width), ref.dtype)

    @pl.when(jnp.logical_not(has_right))
    def _():
        for ref in (c0, p0, m0, lab, c1, p1, m1):
            ref[last, PAD : PAD + layers, :] = jnp.zeros((layers, width), ref.dtype)

    pl.semaphore_wait(barrier, n - 1)

    for j in range(tiles):
        for f in range(4):
            @pl.when(has_left)
            def _():
                halo(0, 0, f, j).start()

            @pl.when(has_right)
            def _():
                halo(0, 1, f, j).start()

    for copy in loads:
        copy.wait()

    def fold(v):
        total = v[:, 0:128]
        for at in range(128, width, 128):
            total = total + v[:, at : at + 128]
        return total

    def soak(labels, m):
        return jnp.where(labels >= 1, 1.0 / (1.0 + m * m), 0.0)

    def exchange(labels, c, p, x, z, shift):
        power = (shift - p) * LOG
        is_wall = labels == 2
        k = jnp.where(is_wall, rate[x - 1, pl.ds(z - PAD, 8), :], 0.0)
        forward = k * c * jnp.exp2(power)
        backward = k * jnp.exp2(-power)
        fwd[x - 1, pl.ds(z - PAD, 8), :] = forward
        bwd[x - 1, pl.ds(z - PAD, 8), :] = backward
        return fold(forward), fold(backward), fold(jnp.where(is_wall, 1.0, 0.0))

    def sum_start(step, sums):
        row = lax.broadcasted_iota(jnp.int32, (8, 128), 0)
        a, b, w = (jnp.sum(s, axis=0, keepdims=True) for s in sums)
        part[step] = jnp.where(row == 0, a, jnp.where(row == 1, b, jnp.where(row == 2, w, 0.0)))

        @pl.loop(1, n)
        def _(d):
            pltpu.make_async_remote_copy(
                src_ref=part.at[step],
                dst_ref=gathered.at[step, d - 1],
                send_sem=part_send.at[step],
                recv_sem=part_recv.at[step],
                device_id=(group, lax.rem(me + d, n)),
                device_id_type=MESH,
            ).start()

    def sum_finish(step):
        all_parts = gathered.at[step]
        pltpu.make_async_copy(all_parts, all_parts, part_recv.at[step]).wait()
        total = part[step] + jnp.sum(gathered[step], axis=0)
        a, b, w = (jnp.sum(total[i : i + 1, :], axis=1, keepdims=True) for i in range(3))
        delta = (density[0] * w + b - a) / (1.5 * (a + b))
        return delta, jnp.exp2(delta * LOG), jnp.exp2(-delta * LOG)

    def spread(src, q, x, i):
        z = PAD + 8 * i
        c_ref, p_ref, m_ref = src
        here = pl.ds(z, 8)
        c, p, m, labels, weight = (r[x, here, :] for r in (c_ref, p_ref, m_ref, lab, q))
        lane = lax.broadcasted_iota(jnp.int32, (8, width), 1)
        near = []
        for at in ((x - 1, here), (x + 1, here), (x, pl.ds(z - 1, 8)), (x, pl.ds(z + 1, 8))):
            near.append(tuple(r[at[0], at[1], :] for r in (c_ref, p_ref, m_ref, lab, q)))
        for shift, edge in ((1, 0), (width - 1, width - 1)):
            cb, pb, mb, lb, qb = (pltpu.roll(v, shift, 1) for v in (c, p, m, labels, weight))
            near.append((cb, pb, mb, jnp.where(lane == edge, 0, lb), jnp.where(lane == edge, 0.0, qb)))
        dc = dp = dm = None
        for cb, pb, mb, lb, qb in near:
            tc = qb * (cb - c)
            tp = jnp.where(lb == 2, pb - p, 0.0)
            tm = jnp.where(lb >= 1, mb - m, 0.0)
            dc, dp, dm = (tc, tp, tm) if dc is None else (dc + tc, dp + tp, dm + tm)
        is_open, is_wall = labels >= 1, labels == 2
        dc = weight * dc
        if i == 0:
            top = lax.broadcasted_iota(jnp.int32, (8, width), 0) == 0
            dm = jnp.where(top, dm - m, dm)
            dc = dc + jnp.where(jnp.logical_and(top, is_open), 1.0 - c, 0.0)
        if i == tiles - 1:
            bottom = lax.broadcasted_iota(jnp.int32, (8, width), 0) == 7
            dp = jnp.where(bottom, dp - p, dp)
        c = c + 0.16 * dc
        p = p + jnp.where(is_wall, 0.15 * dp, 0.0)
        m = m + jnp.where(is_open, 0.12 * dm, 0.0)
        return c, p, m

    def react(values, x, i, up, down):
        c, p, m = values
        z = pl.ds(8 * i, 8)
        reaction = fwd[x - 1, z, :] * up - bwd[x - 1, z, :] * down
        return c - 0.04 * reaction, p - 0.3 * reaction, m + 0.06 * reaction

    def put(dst, x, i, values):
        for ref, value in zip(dst, values):
            ref[x, pl.ds(PAD + 8 * i, 8), :] = value

    def get(src, x, i):
        return tuple(ref[x, pl.ds(PAD + 8 * i, 8), :] for ref in src)

    def add(sums, more):
        return tuple(s + t for s, t in zip(sums, more))

    none = (jnp.zeros((8, 128), jnp.float32),) * 3

    def opening(x, sums):
        for i in range(tiles):
            z = PAD + 8 * i
            c, p, m = get(first, x, i)
            labels = lab[x, pl.ds(z, 8), :]
            q0[x, pl.ds(z, 8), :] = soak(labels, m)
            sums = add(sums, exchange(labels, c, p, x, z, 0.0))
        return sums

    sum_start(0, lax.fori_loop(1, rows + 1, opening, none))

    @pl.loop(2, rows)
    def _(x):
        for i in range(tiles):
            put(second, x, i, spread(first, q0, x, i))

    shift, up, down = sum_finish(0)
    shift_s, up_s, down_s = shift[0, 0], up[0, 0], down[0, 0]

    def settle(values, x, i):
        z = PAD + 8 * i
        c, p, m = react(values, x, i, up_s, down_s)
        put(second, x, i, (c, p, m))
        labels = lab[x, pl.ds(z, 8), :]
        q1[x, pl.ds(z, 8), :] = soak(labels, m)
        return exchange(labels, c, p, x, z, shift_s)

    def inner(x, sums):
        for i in range(tiles):
            sums = add(sums, settle(get(second, x, i), x, i))
        return sums

    sums = lax.fori_loop(2, rows, inner, none)

    sides = ((0, 1, 1, has_left), (last, rows, 0, has_right))
    for i in range(tiles):
        for outer, x, way, present in sides:
            @pl.when(present)
            def _():
                for f in range(4):
                    halo(0, way, f, i).wait_recv()

            z = pl.ds(PAD + 8 * i, 8)
            q0[outer, z, :] = soak(lab[outer, z, :], m0[outer, z, :])
            sums = add(sums, settle(spread(first, q0, x, i), x, i))

            @pl.when(present)
            def _():
                for f in range(3):
                    halo(1, 1 - way, f, i).start()

    sum_start(1, sums)

    @pl.loop(2, rows)
    def _(x):
        for i in range(tiles):
            put(first, x, i, spread(second, q1, x, i))

    _, up, down = sum_finish(1)
    up_f, down_f = up[0, 0], down[0, 0]

    @pl.loop(2, rows)
    def _(x):
        for i in range(tiles):
            put(first, x, i, react(get(first, x, i), x, i, up_f, down_f))

    stores = []
    for f in range(3):
        stores.append(
            pltpu.make_async_copy(
                first[f].at[pl.ds(2, rows - 2), pl.ds(PAD, layers), :],
                outs[f].at[pl.ds(1, rows - 2), :, :],
                store_sem.at[f, 0],
            )
        )
        stores[-1].start()

    for i in range(tiles):
        for outer, x, way, present in sides:
            @pl.when(present)
            def _():
                for f in range(3):
                    halo(1, way, f, i).wait_recv()

            z = pl.ds(PAD + 8 * i, 8)
            q1[outer, z, :] = soak(lab[outer, z, :], m1[outer, z, :])
            put(first, x, i, react(spread(second, q1, x, i), x, i, up_f, down_f))

    for f in range(3):
        for s, x in enumerate((1, rows)):
            stores.append(
                pltpu.make_async_copy(
                    first[f].at[x, pl.ds(PAD, layers), :], outs[f].at[x - 1], store_sem.at[f, 1 + s]
                )
            )
            stores[-1].start()

    for step in range(2):
        pltpu.make_async_copy(gathered.at[step], gathered.at[step], part_send.at[step]).wait()
        for outer, x, way, present in sides:
            @pl.when(present)
            def _():
                for i in range(tiles):
                    for f in range(4 - step):
                        halo(step, 1 - way, f, i).wait_send()
    for copy in stores:
        copy.wait()


def solution(mesh):
    n = mesh.shape["gx"]

    def on_device(oxygen, potential, moisture, rate_constant, cell_labels, current_density):
        rows, layers, width = oxygen.shape
        tiles = layers // 8
        padded = (rows + 2, layers + 2 * PAD, width)
        big = pltpu.VMEM(padded, jnp.float32)
        own = pltpu.VMEM((rows, layers, width), jnp.float32)
        hbm = pl.BlockSpec(memory_space=pl.ANY)
        return pl.pallas_call(
            functools.partial(kernel, n, rows, layers, width),
            out_shape=[jax.ShapeDtypeStruct((rows, layers, width), jnp.float32)] * 3,
            in_specs=[hbm] * 5 + [pl.BlockSpec(memory_space=pltpu.SMEM)],
            out_specs=[hbm] * 3,
            scratch_shapes=[
                big, big, big, big, pltpu.VMEM(padded, jnp.int32),
                big, big, big, big,
                own, own, own,
                pltpu.VMEM((2, 8, 128), jnp.float32),
                pltpu.VMEM((2, n - 1, 8, 128), jnp.float32),
                pltpu.SemaphoreType.DMA((5,)),
                pltpu.SemaphoreType.DMA((3, 3)),
                pltpu.SemaphoreType.DMA((2, 2, 4, tiles)),
                pltpu.SemaphoreType.DMA((2, 2, 4, tiles)),
                pltpu.SemaphoreType.DMA((2,)),
                pltpu.SemaphoreType.DMA((2,)),
            ],
            compiler_params=pltpu.CompilerParams(
                collective_id=0, has_side_effects=True, vmem_limit_bytes=48 * 1024 * 1024
            ),
        )(oxygen, potential, moisture, rate_constant, cell_labels, current_density)

    field = P(("groups", "gx"), None, None)
    return jax.shard_map(
        on_device,
        mesh=mesh,
        in_specs=(field,) * 5 + (P("groups"),),
        out_specs=(field,) * 3,
        check_vma=False,
    )
```

time: 132 us -> 42.1 us (0.32)
  the two profiles are of different devices: /device:TPU:0 before, /device:TPU:9 now
where the time goes in v1:
time: 42.1 us; the launch traced here: 41.9 us
  Pallas kernels  35.2 us (84%)
  local copies, waits for them, and re-layouts  5.35 us (13%)
  between operations  1.3 us (3%)
    pallas_call x1, Pallas kernels, on_device(): pl.pallas_call(functools.partial(kernel, n, rows, layers, width), out_sha...  35.2 us
    unnamed x7, local copies, waits for them, and re-layouts  5.35 us

profile of v1, /device:TPU:9, one launch (start us, length us, event | category | flops | bytes accessed | tf_op | source)
XLA Modules:
  0.0 41.9 jit_solution(8828712061140326862)
XLA Ops:
  1.3 0.0 copy-start
  1.3 1.2 %copy-done = f32[8,32,1024]{2,1,0:T(8,128)S(1)} copy-done((f32[8,32,1024]{2,1,0:T(8,128)S(1)}, f32[8,32,1024]{2,1,0:T(8,128)}, u32[]{:S(2)}) %copy-start) | copy-done | bytes 1048600
  2.5 0.0 copy-start.1
  2.5 1.2 %copy-done.1 = f32[8,32,1024]{2,1,0:T(8,128)S(1)} copy-done((f32[8,32,1024]{2,1,0:T(8,128)S(1)}, f32[8,32,1024]{2,1,0:T(8,128)}, u32[]{:S(2)}) %copy-start.1) | copy-done | bytes 1048600
  3.7 35.2 %shard_map.85 = (f32[8,32,1024]{2,1,0:T(8,128)S(1)}, f32[8,32,1024]{2,1,0:T(8,128)S(1)}, f32[8,32,1024]{2,1,0:T(8,128)S(1)}) custom-call(f32[8,32,1024]{2,1,0:T(8,128)S(1)} %copy-done, f32[8,32,1024]{2,1,0:T(8,128)S(1)} %copy-done.1, f32[8,32,1024]{2,1,0:T(8,128)} %m_in.1, f32[8,32,1024]{2,1,0:T(8,128)} %k_in.1, s32[8,32,1024]{2,1,0:T(8,128)} %l_in.1, ...), custom_call_target="tpu_custom_call" | custom-call | tf_op jit(solution)/shard_map/pallas_call | solution.py:311
  39.0 1.0 %copy.13 = f32[8,32,1024]{2,1,0:T(8,128)} copy(f32[8,32,1024]{2,1,0:T(8,128)S(1)} %get-tuple-element.6) | data formatting | bytes 2097152
  39.9 1.0 %copy.14 = f32[8,32,1024]{2,1,0:T(8,128)} copy(f32[8,32,1024]{2,1,0:T(8,128)S(1)} %get-tuple-element.7) | data formatting | bytes 2097152
  40.9 1.0 %copy.15 = f32[8,32,1024]{2,1,0:T(8,128)} copy(f32[8,32,1024]{2,1,0:T(8,128)S(1)} %get-tuple-element.8) | data formatting | bytes 2097152
Async XLA Ops:
  1.3 1.2 %copy-start = (f32[8,32,1024]{2,1,0:T(8,128)S(1)}, f32[8,32,1024]{2,1,0:T(8,128)}, u32[]{:S(2)}) copy-start(f32[8,32,1024]{2,1,0:T(8,128)} %c_in.1) | copy-start | bytes 3145732
  2.5 1.2 %copy-start.1 = (f32[8,32,1024]{2,1,0:T(8,128)S(1)}, f32[8,32,1024]{2,1,0:T(8,128)}, u32[]{:S(2)}) copy-start(f32[8,32,1024]{2,1,0:T(8,128)} %p_in.1) | copy-start | bytes 3145732

commit v2 on v1

--- a/solution.py
+++ b/solution.py
@@ -11,6 +11,7 @@
 MESH = pl.DeviceIdType.MESH
 LOG = 1.5 * math.log2(math.e)
 PAD = 8
+AHEAD = 2
 
 
 def kernel(
@@ -83,7 +84,7 @@
 
     pl.semaphore_wait(barrier, n - 1)
 
-    for j in range(tiles):
+    def send_rows(j):
         for f in range(4):
             @pl.when(has_left)
             def _():
@@ -92,6 +93,9 @@
             @pl.when(has_right)
             def _():
                 halo(0, 1, f, j).start()
+
+    for j in range(AHEAD):
+        send_rows(j)
 
     for copy in loads:
         copy.wait()
@@ -116,9 +120,9 @@
         return fold(forward), fold(backward), fold(jnp.where(is_wall, 1.0, 0.0))
 
     def sum_start(step, sums):
-        row = lax.broadcasted_iota(jnp.int32, (8, 128), 0)
-        a, b, w = (jnp.sum(s, axis=0, keepdims=True) for s in sums)
-        part[step] = jnp.where(row == 0, a, jnp.where(row == 1, b, jnp.where(row == 2, w, 0.0)))
+        lane = lax.broadcasted_iota(jnp.int32, (1, 128), 1)
+        a, b, w = (jnp.sum(jnp.sum(s, axis=0, keepdims=True), axis=1, keepdims=True) for s in sums)
+        part[step] = jnp.where(lane == 0, a, jnp.where(lane == 1, b, jnp.where(lane == 2, w, 0.0)))
 
         @pl.loop(1, n)
         def _(d):
@@ -135,7 +139,7 @@
         all_parts = gathered.at[step]
         pltpu.make_async_copy(all_parts, all_parts, part_recv.at[step]).wait()
         total = part[step] + jnp.sum(gathered[step], axis=0)
-        a, b, w = (jnp.sum(total[i : i + 1, :], axis=1, keepdims=True) for i in range(3))
+        a, b, w = (total[:, i : i + 1] for i in range(3))
         delta = (density[0] * w + b - a) / (1.5 * (a + b))
         return delta, jnp.exp2(delta * LOG), jnp.exp2(-delta * LOG)
 
@@ -199,6 +203,8 @@
         return sums
 
     sum_start(0, lax.fori_loop(1, rows + 1, opening, none))
+    for j in range(AHEAD, tiles):
+        send_rows(j)
 
     @pl.loop(2, rows)
     def _(x):
@@ -216,15 +222,14 @@
         q1[x, pl.ds(z, 8), :] = soak(labels, m)
         return exchange(labels, c, p, x, z, shift_s)
 
-    def inner(x, sums):
-        for i in range(tiles):
-            sums = add(sums, settle(get(second, x, i), x, i))
-        return sums
-
-    sums = lax.fori_loop(2, rows, inner, none)
-
+    def inner(i, sums):
+        return lax.fori_loop(2, rows, lambda x, s: add(s, settle(get(second, x, i), x, i)), sums)
+
+    sums = none
     sides = ((0, 1, 1, has_left), (last, rows, 0, has_right))
     for i in range(tiles):
+        if i == tiles - 1:
+            sums = inner(i, sums)
         for outer, x, way, present in sides:
             @pl.when(present)
             def _():
@@ -239,6 +244,9 @@
             def _():
                 for f in range(3):
                     halo(1, 1 - way, f, i).start()
+
+        if i < tiles - 1:
+            sums = inner(i, sums)
 
     sum_start(1, sums)
 
@@ -298,6 +306,24 @@
         copy.wait()
 
 
+def hand_out(*refs):
+    sources, targets, held, sem = refs[:3], refs[3:6], refs[6:9], refs[9]
+    q = sources[0].shape[0] // 4
+    todo = []
+    for h in range(4):
+        for f in range(3):
+            piece = pl.ds(h * q, q)
+            a = pltpu.make_async_copy(sources[f].at[piece], held[f].at[piece], sem.at[0, f, h])
+            b = pltpu.make_async_copy(held[f].at[piece], targets[f].at[piece], sem.at[1, f, h])
+            a.start()
+            todo.append((a, b))
+    for a, b in todo:
+        a.wait()
+        b.start()
+    for a, b in todo:
+        b.wait()
+
+
 def solution(mesh):
     n = mesh.shape["gx"]
 
@@ -308,17 +334,18 @@
         big = pltpu.VMEM(padded, jnp.float32)
         own = pltpu.VMEM((rows, layers, width), jnp.float32)
         hbm = pl.BlockSpec(memory_space=pl.ANY)
-        return pl.pallas_call(
+        pinned = pl.BlockSpec(memory_space=pltpu.HBM)
+        fields = pl.pallas_call(
             functools.partial(kernel, n, rows, layers, width),
             out_shape=[jax.ShapeDtypeStruct((rows, layers, width), jnp.float32)] * 3,
-            in_specs=[hbm] * 5 + [pl.BlockSpec(memory_space=pltpu.SMEM)],
+            in_specs=[pinned] * 5 + [pl.BlockSpec(memory_space=pltpu.SMEM)],
             out_specs=[hbm] * 3,
             scratch_shapes=[
                 big, big, big, big, pltpu.VMEM(padded, jnp.int32),
                 big, big, big, big,
                 own, own, own,
-                pltpu.VMEM((2, 8, 128), jnp.float32),
-                pltpu.VMEM((2, n - 1, 8, 128), jnp.float32),
+                pltpu.VMEM((2, 1, 128), jnp.float32),
+                pltpu.VMEM((2, n - 1, 1, 128), jnp.float32),
                 pltpu.SemaphoreType.DMA((5,)),
                 pltpu.SemaphoreType.DMA((3, 3)),
                 pltpu.SemaphoreType.DMA((2, 2, 4, tiles)),
@@ -327,9 +354,17 @@
                 pltpu.SemaphoreType.DMA((2,)),
             ],
             compiler_params=pltpu.CompilerParams(
-                collective_id=0, has_side_effects=True, vmem_limit_bytes=48 * 1024 * 1024
+                collective_id=0, has_side_effects=True, vmem_limit_bytes=63 * 1024 * 1024 + 512 * 1024
             ),
         )(oxygen, potential, moisture, rate_constant, cell_labels, current_density)
+        return pl.pallas_call(
+            hand_out,
+            out_shape=[jax.ShapeDtypeStruct((rows, layers, width), jnp.float32)] * 3,
+            in_specs=[hbm] * 3,
+            out_specs=[pinned] * 3,
+            scratch_shapes=[own, own, own, pltpu.SemaphoreType.DMA((2, 3, 4))],
+            compiler_params=pltpu.CompilerParams(vmem_limit_bytes=62 * 1024 * 1024),
+        )(*fields)
 
     field = P(("groups", "gx"), None, None)
     return jax.shard_map(

time: 42.1 us -> 34.9 us (0.83)
  local copies, waits for them, and re-layouts: 5.35 us -> 0 us
  Pallas kernels: 35.2 us -> 33 us
    unnamed x7 -> x0, local copies, waits for them, and re-layouts: 5.35 us -> none
    pallas_call x1, Pallas kernels: 35.2 us -> 30.2 us  [on_device(): pl.pallas_call(functools.partial(kernel, n, rows, layers, width), out_sha...]
    pallas_call x0 -> x1, Pallas kernels: none -> 2.81 us  [on_device(): pl.pallas_call(hand_out, out_shape=[jax.ShapeDtypeStruct((rows, layers, w...]
where the time goes in v2:
time: 34.9 us; the launch traced here: 34.3 us
  Pallas kernels  33 us (95%)
  between operations  1.29 us (4%)
    pallas_call x1, Pallas kernels, on_device(): pl.pallas_call(functools.partial(kernel, n, rows, layers, width), out_sha...  30.2 us
    pallas_call x1, Pallas kernels, on_device(): pl.pallas_call(hand_out, out_shape=[jax.ShapeDtypeStruct((rows, layers, w...  2.81 us

profile of v2, /device:TPU:9, one launch (start us, length us, event | category | flops | bytes accessed | tf_op | source)
XLA Modules:
  0.0 34.3 jit_solution(16791619702663647796)
XLA Ops:
  1.3 30.2 %shard_map.85 = (f32[8,32,1024]{2,1,0:T(8,128)}, f32[8,32,1024]{2,1,0:T(8,128)}, f32[8,32,1024]{2,1,0:T(8,128)}) custom-call(f32[8,32,1024]{2,1,0:T(8,128)} %c_in.1, f32[8,32,1024]{2,1,0:T(8,128)} %p_in.1, f32[8,32,1024]{2,1,0:T(8,128)} %m_in.1, f32[8,32,1024]{2,1,0:T(8,128)} %k_in.1, s32[8,32,1024]{2,1,0:T(8,128)} %l_in.1, f32[1]{0:T(128)S(6)} %copy.9.density), custom_call_target="tpu_custom_call" | custom-call | tf_op jit(solution)/shard_map/pallas_call | solution.py:338
  31.5 2.8 %shard_map.86 = (f32[8,32,1024]{2,1,0:T(8,128)}, f32[8,32,1024]{2,1,0:T(8,128)}, f32[8,32,1024]{2,1,0:T(8,128)}) custom-call(f32[8,32,1024]{2,1,0:T(8,128)} %get-tuple-element.6.refs_0_, f32[8,32,1024]{2,1,0:T(8,128)} %get-tuple-element.7.refs_1_, f32[8,32,1024]{2,1,0:T(8,128)} %get-tuple-element.8.refs_2_), custom_call_target="tpu_custom_call" | custom-call | tf_op jit(solution)/shard_map/pallas_call | solution.py:360

commit v3 on v2

--- a/solution.py
+++ b/solution.py
@@ -284,15 +284,15 @@
             z = pl.ds(PAD + 8 * i, 8)
             q1[outer, z, :] = soak(lab[outer, z, :], m1[outer, z, :])
             put(first, x, i, react(spread(second, q1, x, i), x, i, up_f, down_f))
-
-    for f in range(3):
-        for s, x in enumerate((1, rows)):
-            stores.append(
-                pltpu.make_async_copy(
-                    first[f].at[x, pl.ds(PAD, layers), :], outs[f].at[x - 1], store_sem.at[f, 1 + s]
+            for f in range(3):
+                stores.append(
+                    pltpu.make_async_copy(
+                        first[f].at[x, z, :],
+                        outs[f].at[x - 1, pl.ds(8 * i, 8), :],
+                        store_sem.at[f, 1 + 2 * i + way],
+                    )
                 )
-            )
-            stores[-1].start()
+                stores[-1].start()
 
     for step in range(2):
         pltpu.make_async_copy(gathered.at[step], gathered.at[step], part_send.at[step]).wait()
@@ -347,7 +347,7 @@
                 pltpu.VMEM((2, 1, 128), jnp.float32),
                 pltpu.VMEM((2, n - 1, 1, 128), jnp.float32),
                 pltpu.SemaphoreType.DMA((5,)),
-                pltpu.SemaphoreType.DMA((3, 3)),
+                pltpu.SemaphoreType.DMA((3, 1 + 2 * tiles)),
                 pltpu.SemaphoreType.DMA((2, 2, 4, tiles)),
                 pltpu.SemaphoreType.DMA((2, 2, 4, tiles)),
                 pltpu.SemaphoreType.DMA((2,)),

time: 34.9 us -> 34.8 us (level)
  no operation moved by 1% of the time
where the time goes in v3:
time: 34.8 us; the launch traced here: 34.2 us
  Pallas kernels  33 us (95%)
  between operations  1.29 us (4%)
    pallas_call x1, Pallas kernels, on_device(): pl.pallas_call(functools.partial(kernel, n, rows, layers, width), out_sha...  30.2 us
    pallas_call x1, Pallas kernels, on_device(): pl.pallas_call(hand_out, out_shape=[jax.ShapeDtypeStruct((rows, layers, w...  2.81 us

profile of v3, /device:TPU:9, one launch (start us, length us, event | category | flops | bytes accessed | tf_op | source)
XLA Modules:
  0.0 34.2 jit_solution(8854149257719736586)
XLA Ops:
  1.3 30.2 %shard_map.85 = (f32[8,32,1024]{2,1,0:T(8,128)}, f32[8,32,1024]{2,1,0:T(8,128)}, f32[8,32,1024]{2,1,0:T(8,128)}) custom-call(f32[8,32,1024]{2,1,0:T(8,128)} %c_in.1, f32[8,32,1024]{2,1,0:T(8,128)} %p_in.1, f32[8,32,1024]{2,1,0:T(8,128)} %m_in.1, f32[8,32,1024]{2,1,0:T(8,128)} %k_in.1, s32[8,32,1024]{2,1,0:T(8,128)} %l_in.1, f32[1]{0:T(128)S(6)} %copy.9.density), custom_call_target="tpu_custom_call" | custom-call | tf_op jit(solution)/shard_map/pallas_call | solution.py:338
  31.4 2.8 %shard_map.86 = (f32[8,32,1024]{2,1,0:T(8,128)}, f32[8,32,1024]{2,1,0:T(8,128)}, f32[8,32,1024]{2,1,0:T(8,128)}) custom-call(f32[8,32,1024]{2,1,0:T(8,128)} %get-tuple-element.6.refs_0_, f32[8,32,1024]{2,1,0:T(8,128)} %get-tuple-element.7.refs_1_, f32[8,32,1024]{2,1,0:T(8,128)} %get-tuple-element.8.refs_2_), custom_call_target="tpu_custom_call" | custom-call | tf_op jit(solution)/shard_map/pallas_call | solution.py:360
